TPU v7x, 32 devices: a whole 2x2x4 slice. The times are simulated.
32 devices in a mesh: fsdp: 16 (over z, y, x), tensor: 2 (over core).
Axes of the slice: x: 2, y: 2, z: 4, core: 2. Of those that a mesh axis runs over, the one named last changes fastest.
Arguments:
- tokens: bfloat16 [50432, 768], P(('fsdp', 'tensor')), may hold values from -6 to 6
- w_qkv: bfloat16 [3, 768, 768], P(None, 'fsdp', 'tensor'), may hold values from -0.21875 to 0.21875
- b_qv: bfloat16 [2, 768], P(None, 'fsdp'), may hold values from -3 to 3
- w_out: bfloat16 [768, 768], P('tensor', 'fsdp'), may hold values from -1.75 to 1.75
- b_out: bfloat16 [768], P('fsdp'), may hold values from -2 to 2
- norm_gains: bfloat16 [2, 768], P(None, 'fsdp'), may hold values from 0.5 to 1.5
- norm_shifts: bfloat16 [2, 768], P(None, 'fsdp'), may hold values from -2 to 2
- w_fc1: bfloat16 [768, 3072], P('fsdp', 'tensor'), may hold values from -0.21875 to 0.21875
- b_fc1: bfloat16 [3072], P('fsdp'), may hold values from -3 to 3
- w_fc2: bfloat16 [3072, 768], P('tensor', 'fsdp'), may hold values from -0.109375 to 0.109375
- b_fc2: bfloat16 [768], P('fsdp'), may hold values from -2 to 2
- cotangent: bfloat16 [50432, 768], P(('fsdp', 'tensor')), may hold values from -6 to 6
Outputs:
- result: bfloat16 [50432, 768], P(('fsdp', 'tensor'))
- grad_tokens: bfloat16 [50432, 768], P(('fsdp', 'tensor'))
- grad_w_qkv: float32 [3, 768, 768], P(None, 'fsdp', 'tensor')
- grad_b_qv: float32 [2, 768], P(None, 'fsdp')
- grad_w_out: float32 [768, 768], P('tensor', 'fsdp')
- grad_b_out: float32 [768], P('fsdp')
- grad_norm_gains: float32 [2, 768], P(None, 'fsdp')
- grad_norm_shifts: float32 [2, 768], P(None, 'fsdp')
- grad_w_fc1: float32 [768, 3072], P('fsdp', 'tensor')
- grad_b_fc1: float32 [3072], P('fsdp')
- grad_w_fc2: float32 [3072, 768], P('tensor', 'fsdp')
- grad_b_fc2: float32 [768], P('fsdp')
All inputs are finite; a program needn't handle non-finite values.
Results may differ from a plain program's by a relative error of at most 0.015.
Values may be sent and summed in bfloat16 or wider, within the bound.
A program may use at most 256 MiB of HBM per device.

v0:
```python
import jax
import jax.numpy as jnp
from jax import lax
from jax.sharding import PartitionSpec as P

HDIM = 64
SEQ = 197


EPS = 1e-06


def layer_norm(value, gain, shift):
    center = value - jnp.mean(value, axis=-1, keepdims=True)
    spread = jnp.mean(center * center, axis=-1, keepdims=True)
    return center * lax.rsqrt(spread + EPS) * gain + shift


def exact_gelu(value):
    return jax.nn.gelu(value, approximate=False)


def body(
    tokens,
    w_qkv,
    b_qv,
    w_out,
    b_out,
    norm_gains,
    norm_shifts,
    w_fc1,
    b_fc1,
    w_fc2,
    b_fc2,
    cotangent,
):
    f32 = jnp.float32
    bf16 = jnp.bfloat16
    parts = lax.axis_size("tensor")
    place = lax.axis_index("tensor")
    rows = tokens.shape[0]
    width = tokens.shape[1]
    shard_cols = w_qkv.shape[2]
    shard_hidden = w_fc1.shape[1]
    scale = HDIM ** (-0.5)
    qkv_full, out_full, bias_qv, bias_out, gains, shifts = (
        lax.all_gather(w_qkv, "fsdp", axis=1, tiled=True),
        lax.all_gather(w_out, "fsdp", axis=1, tiled=True),
        lax.all_gather(b_qv, "fsdp", axis=1, tiled=True),
        lax.all_gather(b_out, "fsdp", axis=0, tiled=True),
        lax.all_gather(norm_gains, "fsdp", axis=1, tiled=True),
        lax.all_gather(norm_shifts, "fsdp", axis=1, tiled=True),
    )
    fc1_full, fc2_full, bias_fc1, bias_fc2 = (
        lax.all_gather(w_fc1, "fsdp", axis=0, tiled=True),
        lax.all_gather(w_fc2, "fsdp", axis=1, tiled=True),
        lax.all_gather(b_fc1, "fsdp", axis=0, tiled=True),
        lax.all_gather(b_fc2, "fsdp", axis=0, tiled=True),
    )
    gains = gains.astype(f32)
    shifts = shifts.astype(f32)
    bias_mine = lax.dynamic_slice_in_dim(bias_qv, place * shard_cols, shard_cols, 1).astype(f32)
    bias_hidden = lax.dynamic_slice_in_dim(bias_fc1, place * shard_hidden, shard_hidden, 0).astype(
        f32
    )
    group_rows = rows * parts
    head_cols = qkv_full.shape[2]
    images = group_rows // SEQ
    heads_here = head_cols // HDIM
    resid = tokens.astype(f32)
    normed1, norm1_back = jax.vjp(layer_norm, resid, gains[0], shifts[0])
    rows1 = lax.all_gather(normed1.astype(bf16), "tensor", axis=0, tiled=True)
    proj = jnp.einsum("td,cdh->cth", rows1, qkv_full, preferred_element_type=f32)
    bias_rows = jnp.stack([bias_mine[0], jnp.zeros((head_cols,), f32), bias_mine[1]])
    qkv = (proj + bias_rows[:, None, :]).astype(bf16)
    shaped = qkv.reshape(3, images, SEQ, heads_here, HDIM)
    query = shaped[0]
    keys = shaped[1]
    values = shaped[2]
    scores = jnp.einsum("ishd,ikhd->ihsk", query, keys, preferred_element_type=f32) * scale
    top = jnp.max(scores, axis=-1, keepdims=True)
    expd = jnp.exp(scores - top)
    total = jnp.sum(expd, axis=-1, keepdims=True)
    probs = expd / total
    log_total = top + jnp.log(total)
    mixed = jnp.einsum("ihsk,ikhd->ishd", probs.astype(bf16), values, preferred_element_type=f32)
    attended = mixed.reshape(group_rows, head_cols).astype(bf16)
    piece = attended
    branch1 = lax.psum_scatter(
        jnp.dot(piece, out_full, preferred_element_type=f32).astype(jnp.bfloat16),
        "tensor",
        scatter_dimension=0,
        tiled=True,
    ).astype(jnp.float32) + bias_out.astype(f32)
    mid = resid + branch1
    normed2, norm2_back = jax.vjp(layer_norm, mid, gains[1], shifts[1])
    rows2 = lax.all_gather(normed2.astype(bf16), "tensor", axis=0, tiled=True)
    hidden = jnp.dot(rows2, fc1_full, preferred_element_type=f32) + bias_hidden
    activ, gelu_back = jax.vjp(exact_gelu, hidden)
    activ_low = activ.astype(bf16)
    piece = activ_low
    branch2 = lax.psum_scatter(
        jnp.dot(piece, fc2_full, preferred_element_type=f32).astype(jnp.bfloat16),
        "tensor",
        scatter_dimension=0,
        tiled=True,
    ).astype(jnp.float32) + bias_fc2.astype(f32)
    result = (mid + branch2).astype(bf16)
    upstream = cotangent.astype(f32)
    back_rows2 = lax.all_gather(cotangent, "tensor", axis=0, tiled=True)
    grad_fc2 = jnp.einsum("tf,td->fd", activ_low, back_rows2, preferred_element_type=f32)
    grad_activ = jnp.einsum("td,fd->tf", back_rows2, fc2_full, preferred_element_type=f32)
    grad_hidden = gelu_back(grad_activ)[0].astype(bf16)
    grad_fc1 = jnp.einsum("td,tf->df", rows2, grad_hidden, preferred_element_type=f32)
    hidden_bias_grad = jnp.sum(grad_hidden.astype(f32), axis=0)
    piece = grad_hidden
    grad_normed2 = lax.psum_scatter(
        jnp.einsum("tf,df->td", piece, fc1_full, preferred_element_type=f32).astype(jnp.bfloat16),
        "tensor",
        scatter_dimension=0,
        tiled=True,
    ).astype(jnp.float32)
    grad_mid_norm, grad_gain2, grad_shift2 = norm2_back(grad_normed2)
    grad_mid = upstream + grad_mid_norm
    grad_branch = grad_mid.astype(bf16)
    back_rows1 = lax.all_gather(grad_branch, "tensor", axis=0, tiled=True)
    grad_out = jnp.einsum("th,td->hd", attended, back_rows1, preferred_element_type=f32)
    grad_attended = jnp.einsum(
        "td,hd->th", back_rows1, out_full, preferred_element_type=f32
    ).astype(bf16)
    grad_mixed = grad_attended.reshape(images, SEQ, heads_here, HDIM)
    again = jnp.einsum("ishd,ikhd->ihsk", query, keys, preferred_element_type=f32) * scale
    probs_again = jnp.exp(again - log_total)
    grad_probs = jnp.einsum("ishd,ikhd->ihsk", grad_mixed, values, preferred_element_type=f32)
    inner = jnp.sum(probs_again * grad_probs, axis=-1, keepdims=True)
    grad_scores = (probs_again * (grad_probs - inner)).astype(bf16)
    grad_query = (
        jnp.einsum("ihsk,ikhd->ishd", grad_scores, keys, preferred_element_type=f32) * scale
    )
    grad_keys = (
        jnp.einsum("ihsk,ishd->ikhd", grad_scores, query, preferred_element_type=f32) * scale
    )
    grad_values = jnp.einsum(
        "ihsk,ishd->ikhd", probs_again.astype(bf16), grad_mixed, preferred_element_type=f32
    )
    grad_qkv = (
        jnp.stack([grad_query, grad_keys, grad_values])
        .reshape(3, group_rows, head_cols)
        .astype(bf16)
    )
    grad_qkv_w = jnp.einsum("td,cth->cdh", rows1, grad_qkv, preferred_element_type=f32)
    qv_bias_grad = jnp.sum(grad_qkv.astype(f32), axis=1)
    piece = grad_qkv
    grad_normed1 = lax.psum_scatter(
        jnp.einsum("cth,cdh->td", piece, qkv_full, preferred_element_type=f32).astype(jnp.bfloat16),
        "tensor",
        scatter_dimension=0,
        tiled=True,
    ).astype(jnp.float32)
    grad_resid_norm, grad_gain1, grad_shift1 = norm1_back(grad_normed1)
    grad_tokens = (grad_mid + grad_resid_norm).astype(bf16)
    width_zero = jnp.zeros((width,), f32)
    query_bias = lax.dynamic_update_slice_in_dim(width_zero, qv_bias_grad[0], place * head_cols, 0)
    value_bias = lax.dynamic_update_slice_in_dim(width_zero, qv_bias_grad[2], place * head_cols, 0)
    fc1_bias = lax.dynamic_update_slice_in_dim(
        jnp.zeros((shard_hidden * parts,), f32), hidden_bias_grad, place * shard_hidden, 0
    )
    small = jnp.stack(
        [
            grad_gain1,
            grad_gain2,
            grad_shift1,
            grad_shift2,
            query_bias,
            value_bias,
            jnp.sum(grad_branch.astype(f32), axis=0),
            jnp.sum(upstream, axis=0),
        ]
    )
    small, fc1_bias = (
        lax.psum(small.astype(jnp.bfloat16), "tensor").astype(jnp.float32),
        lax.psum(fc1_bias.astype(jnp.bfloat16), "tensor").astype(jnp.float32),
    )
    sent_qkv, sent_out, sent_small, sent_bias, sent_fc1, sent_fc2 = (
        lax.psum_scatter(grad_qkv_w, "fsdp", scatter_dimension=1, tiled=True),
        lax.psum_scatter(grad_out, "fsdp", scatter_dimension=1, tiled=True),
        lax.psum_scatter(small, "fsdp", scatter_dimension=1, tiled=True),
        lax.psum_scatter(fc1_bias, "fsdp", scatter_dimension=0, tiled=True),
        lax.psum_scatter(grad_fc1, "fsdp", scatter_dimension=0, tiled=True),
        lax.psum_scatter(grad_fc2, "fsdp", scatter_dimension=1, tiled=True),
    )
    return (
        result,
        grad_tokens,
        sent_qkv,
        sent_small[4:6],
        sent_out,
        sent_small[6],
        sent_small[0:2],
        sent_small[2:4],
        sent_fc1,
        sent_bias,
        sent_fc2,
        sent_small[7],
    )


def solution(mesh):
    placed = (
        P(("fsdp", "tensor"), None),
        P(None, "fsdp", "tensor"),
        P(None, "fsdp"),
        P("tensor", "fsdp"),
        P("fsdp"),
        P(None, "fsdp"),
        P(None, "fsdp"),
        P("fsdp", "tensor"),
        P("fsdp"),
        P("tensor", "fsdp"),
        P("fsdp"),
        P(("fsdp", "tensor"), None),
    )
    return jax.shard_map(
        body,
        mesh=mesh,
        in_specs=placed,
        out_specs=(
            P(("fsdp", "tensor"), None),
            P(("fsdp", "tensor"), None),
            P(None, "fsdp", "tensor"),
            P(None, "fsdp"),
            P("tensor", "fsdp"),
            P("fsdp"),
            P(None, "fsdp"),
            P(None, "fsdp"),
            P("fsdp", "tensor"),
            P("fsdp"),
            P("tensor", "fsdp"),
            P("fsdp"),
        ),
        check_vma=False,
    )
```

profile of v0, /device:TPU:0, one launch (start us, length us, event | category | flops | bytes accessed | tf_op | source)
XLA Modules:
  0.0 1460.5 jit_solution(10152149374076100099)
XLA Ops:
  8.0 42.4 %all-gather = bf16[16,48,2]{1,2,0:T(2,128)(2,1)S(1)} all-gather(bf16[1,48,2]{1,2,0:T(2,128)(2,1)} %bitcast.89), channel_id=1, replica_groups=mesh['fsdp'=16,'tensor'=2] {'fsdp'}, dimensions={0}, use_global_device_ids=true | all-gather | bytes 3264 | tf_op jit(solution)/shard_map/all_gather | solution.py:51
  50.5 35.5 %all-gather.1 = bf16[16,48,2]{1,2,0:T(2,128)(2,1)S(1)} all-gather(bf16[1,48,2]{1,2,0:T(2,128)(2,1)} %bitcast.90), channel_id=1, replica_groups=mesh['fsdp'=16,'tensor'=2] {'fsdp'}, dimensions={0}, use_global_device_ids=true | all-gather | bytes 3264 | tf_op jit(solution)/shard_map/all_gather | solution.py:52
  94.4 37.2 %all-gather.2 = bf16[16,48,2]{1,2,0:T(2,128)(2,1)S(1)} all-gather(bf16[1,48,2]{1,2,0:T(2,128)(2,1)S(1)} %bitcast.91), channel_id=1, replica_groups=mesh['fsdp'=16,'tensor'=2] {'fsdp'}, dimensions={0}, use_global_device_ids=true | all-gather | bytes 3264 | tf_op jit(solution)/shard_map/all_gather | solution.py:49
  131.8 39.1 %all_gather.47 = bf16[384,768]{0,1:T(8,128)(2,1)S(1)} all-gather(bf16[384,48]{0,1:T(8,128)(2,1)S(1)} %copy-done.33), channel_id=1, replica_groups=mesh['fsdp'=16,'tensor'=2] {'fsdp'}, dimensions={1}, use_global_device_ids=true | all-gather | bytes 626688 | tf_op jit(solution)/shard_map/all_gather | solution.py:48
  288.0 73.6 %all-reduce.5 = (bf16[768]{0:T(1024)(128)(2,1)S(1)}, bf16[3072]{0:T(1024)(128)(2,1)S(1)}, bf16[768]{0:T(1024)(128)(2,1)}) all-reduce(bf16[768]{0:T(1024)(128)(2,1)S(1)} %dynamic-update-slice, bf16[3072]{0:T(1024)(128)(2,1)S(1)} %dynamic-update-slice.1, bf16[768]{0:T(1024)(128)(2,1)S(1)} %dynamic-update-slice.2), channel_id=1, replica_groups=mesh['fsdp'=16,'tensor'=2] {'fsdp'}, use_global_device_ids=true, to_apply=%add | all-reduce | flops 4608 | bytes 18432
  380.1 51.5 %multiply_convert_fusion.1 = (bf16[3152,1536]{1,0:T(8,128)(2,1)}, f32[3152,1536]{1,0:T(8,128)}, f32[3152,1536]{1,0:T(8,128)}) fusion(f32[1536]{0:T(1024)S(1)} %dynamic-slice_convert_fusion, bf16[3152,768]{1,0:T(8,128)(2,1)} %all-gather.15.cloned.1.call-done, bf16[768,1536]{1,0:T(8,128)(2,1)} %all-gather.17.cloned.1.call-done), kind=kOutput, calls=%fused_computation.9 | convolution fusion | flops 7756038144 | bytes 55621632 | tf_op jit(solution)/shard_map/dot_general | solution.py:98
  431.7 15.0 %all-gather.19.cloned.1.call-done = bf16[1536,768]{0,1:T(8,128)(2,1)} async-done(((bf16[1536,48]{0,1:T(8,128)(2,1)}), bf16[1536,768]{0,1:T(8,128)(2,1)}) %all-gather.19.cloned.1.call-update) | async-done | bytes 2359312 | tf_op jit(solution)/shard_map/all_gather | solution.py:56
  446.7 15.1 %all-gather.21.cloned.1.call-done = bf16[3152,768]{1,0:T(8,128)(2,1)} async-done(((bf16[1576,768]{1,0:T(8,128)(2,1)}), bf16[3152,768]{1,0:T(8,128)(2,1)}) %all-gather.21.cloned.1.call-update) | async-done | bytes 4841488 | tf_op jit(solution)/shard_map/all_gather | solution.py:110
  461.8 26.4 %convert_reduce_fusion = (bf16[1536]{0:T(1024)(128)(2,1)S(1)}, bf16[3152,1536]{1,0:T(8,128)(2,1)}) fusion(f32[3152,1536]{1,0:T(8,128)} %get-tuple-element.78, f32[3152,1536]{1,0:T(8,128)} %get-tuple-element.95, bf16[3152,768]{1,0:T(8,128)(2,1)} %all-gather.21.cloned.1.call-done, bf16[1536,768]{0,1:T(8,128)(2,1)} %all-gather.19.cloned.1.call-done), kind=kOutput, calls=%fused_computation.7 | convolution fusion | flops 7513963008 | bytes 55618560 | tf_op jit(solution)/shard_map/td,fd->tf/dot_general | solution.py:112
  488.2 13.4 convolution_convert_fusion.1
  503.3 13.2 convolution_convert_fusion.2
  543.7 15.5 %all-gather.23.cloned.1.call-done = bf16[3152,768]{1,0:T(8,128)(2,1)} async-done(((bf16[1576,768]{1,0:T(8,128)(2,1)}), bf16[3152,768]{1,0:T(8,128)(2,1)}) %all-gather.23.cloned.1.call-update) | async-done | bytes 4841488 | tf_op jit(solution)/shard_map/all_gather | solution.py:126
  582.1 13.0 convert_bitcast_fusion
  595.1 15.6 %multiply_reduce_fusion = (f32[16,6,197]{2,1,0:T(8,128)S(1)}, f32[16,6,197,197]{2,3,1,0:T(8,128)}) fusion(f32[16,6,197,197]{2,3,1,0:T(8,128)} %get-tuple-element.94, f32[16,6,197]{2,1,0:T(8,128)S(1)} %log_add_fusion, bf16[16,197,6,64]{1,3,2,0:T(8,128)(2,1)} %copy.104, bf16[16,197,6,64]{1,3,2,0:T(8,128)(2,1)} %copy.100), kind=kOutput, calls=%fused_computation.2 | convolution fusion | flops 491768736 | bytes 34798080 | tf_op jit(solution)/shard_map/ishd,ikhd->ihsk/dot_general | solution.py:134
  610.7 18.3 %multiply_convert_fusion = bf16[16,6,197,197]{2,3,1,0:T(8,128)(2,1)} fusion(f32[16,6,197,197]{2,3,1,0:T(8,128)} %get-tuple-element.97, f32[16,6,197,197]{2,3,1,0:T(8,128)} %get-tuple-element.94, f32[16,6,197]{2,1,0:T(8,128)S(1)} %get-tuple-element.96, f32[16,6,197]{2,1,0:T(8,128)S(1)} %log_add_fusion), kind=kLoop, calls=%fused_computation.1 | loop fusion | flops 18628320 | bytes 37407936 | tf_op jit(solution)/shard_map/convert_element_type | solution.py:136
  713.8 12.7 fusion.40
  752.9 13.9 fusion.57
  767.2 13.8 fusion.58
  789.4 125.4 %all-reduce.9.cloned.1.call-done = f32[3,768,384]{2,0,1:T(4,128)} async-done(((f32[3,768,384]{2,0,1:T(4,128)}), f32[3,768,384]{2,0,1:T(4,128)}) %all-reduce.9.cloned.1.call-update) | async-done | bytes 3538960
  916.5 74.7 %all-reduce.4 = f32[3072]{0:T(1024)S(1)} all-reduce(bf16[3072]{0:T(1024)(128)(2,1)S(1)} %get-tuple-element.72), channel_id=10, replica_groups=mesh['fsdp'=16,'tensor'=2] {'fsdp'}, use_global_device_ids=true, to_apply=%region_29.0.clone | all-reduce | flops 3072 | bytes 18432
  997.9 43.0 %reduce-scatter.25.cloned.1.call-done = f32[48,8]{1,0:T(8,128)} async-done(((f32[768,8]{1,0:T(8,128)}), f32[48,8]{1,0:T(8,128)}) %reduce-scatter.25.cloned.1.call-update) | async-done | bytes 1552
  1045.7 137.2 %reduce-scatter.21.cloned.1.call-done = f32[48,1536]{1,0:T(8,128)} async-done(((f32[768,1536]{1,0:T(8,128)}), f32[48,1536]{1,0:T(8,128)}) %reduce-scatter.21.cloned.1.call-update) | async-done | bytes 294928 | tf_op jit(solution)/shard_map/reduce_scatter | solution.py:189
  1182.9 142.7 %reduce-scatter.23.cloned.1.call-done = f32[1536,48]{0,1:T(8,128)} async-done(((f32[1536,768]{0,1:T(8,128)}), f32[1536,48]{0,1:T(8,128)}) %reduce-scatter.23.cloned.1.call-update) | async-done | bytes 294928 | tf_op jit(solution)/shard_map/reduce_scatter | solution.py:190
  1325.7 127.9 %reduce-scatter.19.cloned.1.call-done = f32[384,48]{0,1:T(8,128)} async-done(((f32[384,768]{0,1:T(8,128)}), f32[384,48]{0,1:T(8,128)}) %reduce-scatter.19.cloned.1.call-update) | async-done | bytes 73744 | tf_op jit(solution)/shard_map/reduce_scatter | solution.py:186
  (228 shorter events, 326.9 us)
Async XLA Ops:
  7.2 84.9 %copy-start = (bf16[1576,768]{1,0:T(8,128)(2,1)S(1)}, bf16[1576,768]{1,0:T(8,128)(2,1)}, u32[]{:S(2)}) copy-start(bf16[1576,768]{1,0:T(8,128)(2,1)} %param.12) | copy-start | bytes 7262212
  7.2 163.7 %all-gather.13.cloned.1.call-start = ((), (), s32[]{:S(2)}) async-start(), calls=%async_computation.9 | async-start | bytes 1880064 | tf_op jit(solution)/shard_map/all_gather | solution.py:47
  7.9 163.0 %all-gather.11.cloned.1.call-start = ((), (), s32[]{:S(2)}) async-start(), calls=%async_computation.8 | async-start | bytes 7262208 | tf_op jit(solution)/shard_map/all_gather | solution.py:72
  86.1 280.0 %copy-start.31 = (f32[768]{0:T(1024)}, f32[768]{0:T(1024)S(1)}, u32[]{:S(2)}) copy-start(f32[768]{0:T(1024)S(1)} %get-tuple-element.65) | copy-start | bytes 9220
  88.3 43.5 %copy-start.33 = (bf16[384,48]{0,1:T(8,128)(2,1)S(1)}, bf16[384,48]{0,1:T(8,128)(2,1)}, u32[]{:S(2)}) copy-start(bf16[384,48]{0,1:T(8,128)(2,1)} %param.15) | copy-start | bytes 110596
  94.3 267.3 %reduce-scatter.11.cloned.1.call-start = ((), (), s32[]{:S(2)}) async-start(), calls=%async_computation.10 | async-start | bytes 7262208 | tf_op jit(solution)/shard_map/reduce_scatter | solution.py:89
  170.9 107.1 %copy-start.11 = (bf16[384,768]{0,1:T(8,128)(2,1)}, bf16[384,768]{0,1:T(8,128)(2,1)S(1)}, u32[]{:S(2)}) copy-start(bf16[384,768]{0,1:T(8,128)(2,1)S(1)} %all_gather.47) | copy-start | bytes 1769476
  245.0 11.8 copy-start.9
  256.8 10.6 copy-start.13
  284.7 86.2 %all-gather.17.cloned.1.call-start = ((), (), s32[]{:S(2)}) async-start(), calls=%async_computation.12 | async-start | bytes 2506752 | tf_op jit(solution)/shard_map/all_gather | solution.py:55
  285.3 94.8 %all-gather.15.cloned.1.call-start = ((), (), s32[]{:S(2)}) async-start(), calls=%async_computation.11 | async-start | bytes 7262208 | tf_op jit(solution)/shard_map/all_gather | solution.py:97
  369.5 77.2 %all-gather.19.cloned.1.call-start = ((), (), s32[]{:S(2)}) async-start(), calls=%async_computation.13 | async-start | bytes 2506752 | tf_op jit(solution)/shard_map/all_gather | solution.py:56
  370.0 91.7 %all-gather.21.cloned.1.call-start = ((), (), s32[]{:S(2)}) async-start(), calls=%async_computation.15 | async-start | bytes 7262208 | tf_op jit(solution)/shard_map/all_gather | solution.py:110
  370.8 146.3 %reduce-scatter.15.cloned.1.call-start = ((), (), s32[]{:S(2)}) async-start(), calls=%async_computation.16 | async-start | bytes 7262208 | tf_op jit(solution)/shard_map/reduce_scatter | solution.py:117
  461.8 26.4 %copy-start.37 = (bf16[768,1536]{1,0:T(8,128)(2,1)S(1)}, bf16[768,1536]{1,0:T(8,128)(2,1)}, u32[]{:S(2)}) copy-start(bf16[768,1536]{1,0:T(8,128)(2,1)} %all-gather.17.cloned.1.call-done) | copy-start | bytes 7077892
  501.6 31.2 %reduce-scatter.13.cloned.1.call-start = ((), (), s32[]{:S(2)}) async-start(), calls=%async_computation.14 | async-start | bytes 7262208 | tf_op jit(solution)/shard_map/reduce_scatter | solution.py:102
  516.5 42.7 %all-gather.23.cloned.1.call-start = ((), (), s32[]{:S(2)}) async-start(), calls=%async_computation.17 | async-start | bytes 7262208 | tf_op jit(solution)/shard_map/all_gather | solution.py:126
  540.2 19.0 %copy-start.12 = (bf16[384,768]{0,1:T(8,128)(2,1)S(1)}, bf16[384,768]{0,1:T(8,128)(2,1)}, u32[]{:S(2)}) copy-start(bf16[384,768]{0,1:T(8,128)(2,1)} %copy-done.11) | copy-start | bytes 1769476
  543.2 196.6 %reduce-scatter.17.cloned.1.call-start = ((), (), s32[]{:S(2)}) async-start(), calls=%async_computation.18 | async-start | bytes 7262208 | tf_op jit(solution)/shard_map/reduce_scatter | solution.py:154
  713.7 201.1 %all-reduce.9.cloned.1.call-start = ((), (), s32[]{:S(2)}) async-start(), calls=%async_computation.23 | async-start | bytes 9437184
  732.8 308.0 %reduce-scatter.25.cloned.1.call-start = ((), (), s32[]{:S(2)}) async-start(), calls=%async_computation.22 | async-start | bytes 417792
  752.9 430.1 %reduce-scatter.21.cloned.1.call-start = ((), (), s32[]{:S(2)}) async-start(), calls=%async_computation.20 | async-start | bytes 5013504 | tf_op jit(solution)/shard_map/reduce_scatter | solution.py:189
  766.9 558.8 %reduce-scatter.23.cloned.1.call-start = ((), (), s32[]{:S(2)}) async-start(), calls=%async_computation.21 | async-start | bytes 5013504 | tf_op jit(solution)/shard_map/reduce_scatter | solution.py:190
  781.0 672.5 %reduce-scatter.19.cloned.1.call-start = ((), (), s32[]{:S(2)}) async-start(), calls=%async_computation.19 | async-start | bytes 1253376 | tf_op jit(solution)/shard_map/reduce_scatter | solution.py:186
  (35 other events, 112.3 us)
Sparse Core Ops, SparseCore 0:
  10.7 61.6 all-gather.12
  94.4 12.3 all-gather.10
  284.8 10.3 reduce-scatter.10
  298.3 63.7 all-gather.16
  369.6 10.4 all-gather.14
  383.1 63.5 all-gather.18
  448.3 13.4 all-gather.20
  501.7 14.2 reduce-scatter.14
  518.4 14.3 reduce-scatter.12
  543.3 15.9 all-gather.22
  713.8 14.2 reduce-scatter.16
  733.7 181.0 all-reduce.8
  920.1 120.6 reduce-scatter.24
  1046.4 136.4 reduce-scatter.20
  1189.4 136.2 reduce-scatter.22
  1330.8 122.6 reduce-scatter.18
where the time goes:
time: 1470 us; the launch traced here: 1460 us
  waiting for transfers between devices  643 us (44%)
  blocking collectives  306 us (21%)
  matrix products  252 us (17%)
  local copies, waits for them, and re-layouts  160 us (11%)
  other arithmetic  80 us (5%)
  between operations  17.6 us (1%)
    unnamed x18, waiting for transfers between devices  171 us
    unnamed x2, blocking collectives  148 us
    reduce_scatter x1, waiting for transfers between devices, body(): lax.psum_scatter(grad_fc2, 'fsdp', scatter_dimension=1, tiled=True)  143 us
    reduce_scatter x1, waiting for transfers between devices, body(): lax.psum_scatter(grad_fc1, 'fsdp', scatter_dimension=0, tiled=True)  137 us
    reduce_scatter x1, waiting for transfers between devices, body(): lax.psum_scatter(grad_out, 'fsdp', scatter_dimension=1, tiled=True)  128 us
    another operation x7, local copies, waits for them, and re-layouts, body(): jnp.stack([grad_query, grad_keys, grad_values])  51.9 us
    dot_general x1, matrix products, body(): hidden = jnp.dot(rows2, fc1_full, preferred_element_type=f32) + bias_hidden  51.5 us
    all_gather x1, blocking collectives, body(): lax.all_gather(norm_gains, 'fsdp', axis=1, tiled=True)  42.4 us
  transfers between devices with their start and end apart: 16, of which 10 were waited for; matrix products, arithmetic and copies ran while one was open for 12% of the time, Pallas kernels for 0%

commit v1 on v0

v1 whole, which is shorter than its diff:
```python
import jax
import jax.numpy as jnp
from jax import lax
from jax.experimental import pallas as pl
from jax.experimental.pallas import tpu as pltpu
from jax.sharding import PartitionSpec as P

HDIM = 64
SEQ = 197
PAD = 208
EPS = 1e-06
LANES = 128
F32 = jnp.float32
BF16 = jnp.bfloat16

NT = (((1,), (1,)), ((), ()))
TN = (((0,), (0,)), ((), ()))
NN = (((1,), (0,)), ((), ()))


def mm(a, b, dims):
    return lax.dot_general(a, b, dims, preferred_element_type=F32)


def pair_masks():
    lane = lax.broadcasted_iota(jnp.int32, (1, LANES), 1)
    low = lane < HDIM
    scale = HDIM ** (-0.5)
    picks = (
        jnp.where(low, 1.0, 0.0).astype(BF16),
        jnp.where(low, 0.0, 1.0).astype(BF16),
    )
    scaled = (
        jnp.where(low, scale, 0.0).astype(BF16),
        jnp.where(low, 0.0, scale).astype(BF16),
    )
    return low, picks, scaled


def attend_kernel(own_ref, other_ref, att_ref, lse_ref):
    cols = own_ref.shape[2] // 3
    low, _, scaled = pair_masks()
    real = lax.broadcasted_iota(jnp.int32, (PAD, 1), 0) < SEQ
    lse_ref[...] = jnp.zeros_like(lse_ref)
    head = 0
    for side, ref in enumerate((own_ref, other_ref)):
        for start in range(0, cols, LANES):
            query = ref[0, :, start : start + LANES]
            keys = ref[0, :, cols + start : cols + start + LANES]
            values = ref[0, :, 2 * cols + start : 2 * cols + start + LANES]
            mixed = []
            for part in range(2):
                scores = mm(keys * scaled[part], query, NT)
                scores = jnp.where(real, scores, -1e30)
                top = jnp.max(scores, axis=0, keepdims=True)
                expd = jnp.exp(scores - top)
                total = jnp.sum(expd, axis=0, keepdims=True)
                probs = (expd * (1.0 / total)).astype(BF16)
                lse_ref[0, head : head + 1, :] = top + jnp.log(total)
                mixed.append(mm(probs, values, TN))
                head += 1
            at = side * cols + start
            att_ref[0, :, at : at + LANES] = jnp.where(low, mixed[0], mixed[1]).astype(BF16)


def attend_back_kernel(own_ref, other_ref, grad_ref, lse_ref, gown_ref, gother_ref):
    cols = own_ref.shape[2] // 3
    low, picks, scaled = pair_masks()
    scale = HDIM ** (-0.5)
    real = lax.broadcasted_iota(jnp.int32, (PAD, 1), 0) < SEQ
    head = 0
    for side, (ref, out) in enumerate(((own_ref, gown_ref), (other_ref, gother_ref))):
        for start in range(0, cols, LANES):
            query = ref[0, :, start : start + LANES]
            keys = ref[0, :, cols + start : cols + start + LANES]
            values = ref[0, :, 2 * cols + start : 2 * cols + start + LANES]
            at = side * cols + start
            grad = grad_ref[0, :, at : at + LANES]
            gq, gk, gv = [], [], []
            for part in range(2):
                keys_part = keys * scaled[part]
                scores = mm(keys_part, query, NT)
                probs = jnp.where(real, jnp.exp(scores - lse_ref[0, head : head + 1, :]), 0.0)
                gprobs = mm(values * picks[part], grad, NT)
                inner = jnp.sum(probs * gprobs, axis=0, keepdims=True)
                gscores = (probs * (gprobs - inner)).astype(BF16)
                gq.append(mm(gscores, keys_part, TN))
                gk.append(mm(gscores, query, NN))
                gv.append(mm(probs.astype(BF16), grad, NN))
                head += 1
            out[0, :, start : start + LANES] = (gq[0] + gq[1]).astype(BF16)
            out[0, :, cols + start : cols + start + LANES] = (
                jnp.where(low, gk[0], gk[1]) * scale
            ).astype(BF16)
            out[0, :, 2 * cols + start : 2 * cols + start + LANES] = jnp.where(
                low, gv[0], gv[1]
            ).astype(BF16)


def image_block(rows, cols):
    return pl.BlockSpec((1, rows, cols), lambda i: (i, 0, 0))


def attend(own, other):
    images, _, width = own.shape
    cols = width // 3
    heads = 2 * cols // HDIM
    lse_rows = -(-heads // 8) * 8
    return pl.pallas_call(
        attend_kernel,
        grid=(images,),
        in_specs=[image_block(PAD, width)] * 2,
        out_specs=[image_block(PAD, 2 * cols), image_block(lse_rows, PAD)],
        out_shape=[
            jax.ShapeDtypeStruct((images, PAD, 2 * cols), BF16),
            jax.ShapeDtypeStruct((images, lse_rows, PAD), F32),
        ],
        compiler_params=pltpu.CompilerParams(vmem_limit_bytes=32 * 1024 * 1024),
        cost_estimate=pl.CostEstimate(
            flops=images * heads * PAD * PAD * 64 * 4 * 4,
            bytes_accessed=images * PAD * 8 * cols * 2,
            transcendentals=images * heads * PAD * PAD,
        ),
    )(own, other)


def attend_back(own, other, grad, lse):
    images, _, width = own.shape
    cols = width // 3
    heads = 2 * cols // HDIM
    return pl.pallas_call(
        attend_back_kernel,
        grid=(images,),
        in_specs=[image_block(PAD, width)] * 2
        + [image_block(PAD, 2 * cols), image_block(lse.shape[1], PAD)],
        out_specs=[image_block(PAD, width)] * 2,
        out_shape=[jax.ShapeDtypeStruct((images, PAD, width), BF16)] * 2,
        compiler_params=pltpu.CompilerParams(vmem_limit_bytes=32 * 1024 * 1024),
        cost_estimate=pl.CostEstimate(
            flops=images * heads * PAD * PAD * 64 * 10 * 4,
            bytes_accessed=images * PAD * 14 * cols * 2,
            transcendentals=images * heads * PAD * PAD,
        ),
    )(own, other, grad, lse)


def normalize(value):
    center = value - jnp.mean(value, axis=-1, keepdims=True)
    spread = jnp.mean(center * center, axis=-1, keepdims=True)
    inv = lax.rsqrt(spread + EPS)
    return center * inv, inv


def norm_grad(grad, gain, xhat, inv):
    dx = grad * gain
    return inv * (
        dx - jnp.mean(dx, axis=-1, keepdims=True) - xhat * jnp.mean(dx * xhat, axis=-1, keepdims=True)
    )


def swap(value):
    return lax.ppermute(value, "tensor", [(0, 1), (1, 0)])


def body(
    tokens,
    w_qkv,
    b_qv,
    w_out,
    b_out,
    norm_gains,
    norm_shifts,
    w_fc1,
    b_fc1,
    w_fc2,
    b_fc2,
    cotangent,
):
    parts = lax.axis_size("tensor")
    assert parts == 2
    place = lax.axis_index("tensor")
    rows, width = tokens.shape
    depth = w_qkv.shape[1]
    cols = w_qkv.shape[2]
    units = w_fc1.shape[1]
    images = rows // SEQ
    per_row = b_fc1.shape[0] // depth

    small_in = jnp.concatenate(
        [norm_gains, norm_shifts, b_qv, b_out[None], b_fc2[None], b_fc1.reshape(depth, per_row).T],
        axis=0,
    ).T
    count = small_in.shape[1]
    small_in = jnp.pad(small_in, ((0, 0), (0, LANES - count)))
    panel = jnp.concatenate([w_qkv[0], w_qkv[1], w_qkv[2], w_out.T, small_in], axis=1)
    panel = lax.all_gather(panel, "fsdp", axis=0, tiled=True)
    mlp_own = lax.all_gather(
        jnp.concatenate([w_fc1, w_fc2.T], axis=1), "fsdp", axis=0, tiled=True
    )
    attn_cols = 4 * cols
    qkv_w = [panel[:, : 3 * cols]]
    attn_other = swap(panel[:, :attn_cols])
    qkv_w.append(attn_other[:, : 3 * cols])
    mlp_other = swap(mlp_own)
    fc1 = [mlp_own[:, :units], mlp_other[:, :units]]
    fc2 = [mlp_own[:, units:], mlp_other[:, units:]]
    out_t = jnp.concatenate([panel[:, 3 * cols : attn_cols], attn_other[:, 3 * cols :]], axis=1)
    small_full = panel[:, attn_cols : attn_cols + count].astype(F32).T
    gains, shifts, bias_qv = small_full[0:2], small_full[2:4], small_full[4:6]
    bias_out, bias_fc2 = small_full[6], small_full[7]
    bias_fc1 = small_full[8 : 8 + per_row].T.reshape(-1)

    def halves(vector, size):
        return [
            lax.dynamic_slice_in_dim(vector, place * size, size, 0),
            lax.dynamic_slice_in_dim(vector, (1 - place) * size, size, 0),
        ]

    def joined(own, other):
        return jnp.where(
            place == 0, jnp.concatenate([own, other]), jnp.concatenate([other, own])
        )

    bias_q, bias_v = halves(bias_qv[0], cols), halves(bias_qv[1], cols)
    bias_hidden = halves(bias_fc1, units)

    def padded(value):
        return jnp.pad(
            value.reshape(images, SEQ, width), ((0, 0), (0, PAD - SEQ), (0, 0))
        ).reshape(images * PAD, width)

    def cut(value):
        return value.reshape(images, PAD, width)[:, :SEQ].reshape(rows, width)

    resid = padded(tokens).astype(F32)
    cot = padded(cotangent)
    xhat1, inv1 = normalize(resid)
    normed1 = (xhat1 * gains[0] + shifts[0]).astype(BF16)
    qkv = []
    for p in range(2):
        bias = jnp.concatenate([bias_q[p], jnp.zeros((cols,), F32), bias_v[p]])
        qkv.append(
            (mm(normed1, qkv_w[p], NN) + bias).astype(BF16).reshape(images, PAD, 3 * cols)
        )
    attended, lse = attend(qkv[0], qkv[1])
    attended = attended.reshape(images * PAD, 2 * cols)
    mid = resid + (mm(attended, out_t, NT) + bias_out)
    xhat2, inv2 = normalize(mid)
    normed2 = (xhat2 * gains[1] + shifts[1]).astype(BF16)
    activ, slope = [], []
    for p in range(2):
        hidden = mm(normed2, fc1[p], NN) + bias_hidden[p]
        cdf = 0.5 * (1.0 + lax.erf(hidden * (2.0**-0.5)))
        pdf = jnp.exp(-0.5 * hidden * hidden) * 0.3989422804014327
        activ.append((hidden * cdf).astype(BF16))
        slope.append((cdf + hidden * pdf).astype(BF16))
    result = (mid + (mm(activ[0], fc2[0], NT) + mm(activ[1], fc2[1], NT) + bias_fc2)).astype(BF16)

    grad_fc2 = [mm(cot, activ[p], TN) for p in range(2)]
    total_fc2 = (grad_fc2[0] + swap(grad_fc2[1].astype(BF16)).astype(F32)).astype(BF16)
    grad_hidden = [
        (mm(cot, fc2[p], NN) * slope[p].astype(F32)).astype(BF16) for p in range(2)
    ]
    grad_normed2 = mm(grad_hidden[0], fc1[0], NT) + mm(grad_hidden[1], fc1[1], NT)
    grad_fc1 = [mm(normed2, grad_hidden[p], TN) for p in range(2)]
    total_fc1 = (grad_fc1[0] + swap(grad_fc1[1].astype(BF16)).astype(F32)).astype(BF16)
    sent_mlp = lax.psum_scatter(
        jnp.concatenate([total_fc1, total_fc2], axis=1), "fsdp", scatter_dimension=0, tiled=True
    )
    hidden_sums = [jnp.sum(grad_hidden[p].astype(F32), axis=0) for p in range(2)]

    upstream = cot.astype(F32)
    grad_mid = upstream + norm_grad(grad_normed2, gains[1], xhat2, inv2)
    grad_branch = grad_mid.astype(BF16)
    grad_attended = mm(grad_branch, out_t, NN).astype(BF16)
    grad_out_t = mm(grad_branch, attended, TN)
    grad_qkv = attend_back(
        qkv[0], qkv[1], grad_attended.reshape(images, PAD, 2 * cols), lse
    )
    grad_qkv = [g.reshape(images * PAD, 3 * cols) for g in grad_qkv]
    grad_qkv_w = [mm(normed1, g, TN) for g in grad_qkv]
    qkv_sums = [jnp.sum(g.astype(F32), axis=0) for g in grad_qkv]
    grad_normed1 = mm(grad_qkv[0], qkv_w[0], NT) + mm(grad_qkv[1], qkv_w[1], NT)
    grad_tokens = (grad_mid + norm_grad(grad_normed1, gains[0], xhat1, inv1)).astype(BF16)

    small = jnp.concatenate(
        [
            jnp.stack(
                [
                    jnp.sum(grad_normed1 * xhat1, axis=0),
                    jnp.sum(grad_normed2 * xhat2, axis=0),
                    jnp.sum(grad_normed1, axis=0),
                    jnp.sum(grad_normed2, axis=0),
                    joined(qkv_sums[0][:cols], qkv_sums[1][:cols]),
                    joined(qkv_sums[0][2 * cols :], qkv_sums[1][2 * cols :]),
                    jnp.sum(grad_branch.astype(F32), axis=0),
                    jnp.sum(upstream, axis=0),
                ]
            ),
            joined(hidden_sums[0], hidden_sums[1]).reshape(width, per_row).T,
        ],
        axis=0,
    ).T
    small = jnp.pad(small, ((0, 0), (0, LANES - count))).astype(BF16)
    away = jnp.concatenate(
        [grad_qkv_w[1].astype(BF16), grad_out_t[:, cols:].astype(BF16), small], axis=1
    )
    home = jnp.concatenate([grad_qkv_w[0], grad_out_t[:, :cols], small.astype(F32)], axis=1)
    total = (home + swap(away).astype(F32)).astype(BF16)
    sent = lax.psum_scatter(total, "fsdp", scatter_dimension=0, tiled=True).astype(F32)
    sent_qkv = jnp.stack([sent[:, i * cols : (i + 1) * cols] for i in range(3)])
    sent_small = sent[:, attn_cols : attn_cols + count].T
    return (
        cut(result),
        cut(grad_tokens),
        sent_qkv,
        sent_small[4:6],
        sent[:, 3 * cols : attn_cols].T,
        sent_small[6],
        sent_small[0:2],
        sent_small[2:4],
        sent_mlp[:, :units].astype(F32),
        sent_small[8 : 8 + per_row].T.reshape(-1),
        sent_mlp[:, units:].astype(F32).T,
        sent_small[7],
    )


def solution(mesh):
    both = P(("fsdp", "tensor"), None)
    placed = (
        both,
        P(None, "fsdp", "tensor"),
        P(None, "fsdp"),
        P("tensor", "fsdp"),
        P("fsdp"),
        P(None, "fsdp"),
        P(None, "fsdp"),
        P("fsdp", "tensor"),
        P("fsdp"),
        P("tensor", "fsdp"),
        P("fsdp"),
        both,
    )
    return jax.shard_map(
        body,
        mesh=mesh,
        in_specs=placed,
        out_specs=(
            both,
            both,
            P(None, "fsdp", "tensor"),
            P(None, "fsdp"),
            P("tensor", "fsdp"),
            P("fsdp"),
            P(None, "fsdp"),
            P(None, "fsdp"),
            P("fsdp", "tensor"),
            P("fsdp"),
            P("tensor", "fsdp"),
            P("fsdp"),
        ),
        check_vma=False,
    )
```

time: 1470 us -> 584 us (0.40)
  waiting for transfers between devices: 643 us -> 303 us
  blocking collectives: 306 us -> 0 us
  local copies, waits for them, and re-layouts: 160 us -> 39.4 us
  matrix products: 252 us -> 146 us
  other arithmetic: 80 us -> 30.9 us
  Pallas kernels: 0 us -> 42.7 us
    reduce_scatter x7 -> x2, waiting for transfers between devices: 417 us -> 206 us  [the longest x1 137 us: body(): lax.psum_scatter(jnp.concatenate([total_fc1, total_fc2], axis=1), 'fsdp',...]
    unnamed x18 -> x4, waiting for transfers between devices: 171 us -> 0.07 us
    all_gather x4 -> x0, blocking collectives: 154 us -> none  [the longest x1 42.4 us: body(): lax.all_gather(norm_gains, 'fsdp', axis=1, tiled=True)]
    unnamed x2 -> x0, blocking collectives: 148 us -> none
    dot_general x18 -> x21, matrix products: 252 us -> 146 us  [mm(): return lax.dot_general(a, b, dims, preferred_element_type=F32)]
    another operation x11 -> x7, local copies, waits for them, and re-layouts: 52 us -> 0.61 us  [the longest x6 0.61 us: body(): jnp.stack([jnp.sum(grad_normed1 * xhat1, axis=0), jnp.sum(grad_normed2 *...]
    squeeze x6 -> x0, local copies, waits for them, and re-layouts: 49.3 us -> none  [the longest x2 16.5 us: body(): values = shaped[2]]
    pallas_call x0 -> x2, Pallas kernels: none -> 42.7 us  [the longest x1 29.9 us: attend_back(): pl.pallas_call(attend_back_kernel, grid=(images,), in_specs=[image_block(...]
  transfers between devices with their start and end apart: 16 -> 9, of which waited for: 10 -> 5; matrix products, arithmetic and copies ran while one was open for 12% -> 24% of each run, Pallas kernels for 0% -> 2%
where the time goes in v1:
time: 584 us; the launch traced here: 578 us
  waiting for transfers between devices  303 us (52%)
  matrix products  146 us (25%)
  Pallas kernels  42.7 us (7%)
  local copies, waits for them, and re-layouts  39.4 us (7%)
  other arithmetic  30.9 us (5%)
  between operations  14.8 us (3%)
    dot_general x21, matrix products, mm(): return lax.dot_general(a, b, dims, preferred_element_type=F32)  146 us
    reduce_scatter x1, waiting for transfers between devices, body(): lax.psum_scatter(jnp.concatenate([total_fc1, total_fc2], axis=1), 'fsdp',...  137 us
    reduce_scatter x1, waiting for transfers between devices, body(): lax.psum_scatter(total, 'fsdp', scatter_dimension=0, tiled=True).astype(F32)  69.4 us
    all_gather x1, waiting for transfers between devices, body(): panel = lax.all_gather(panel, 'fsdp', axis=0, tiled=True)  56 us
    all_gather x1, waiting for transfers between devices, body(): lax.all_gather(jnp.concatenate([w_fc1, w_fc2.T], axis=1), 'fsdp', axis=0,...  40.3 us
    pallas_call x1, Pallas kernels, attend_back(): pl.pallas_call(attend_back_kernel, grid=(images,), in_specs=[image_block(...  29.9 us
    pallas_call x1, Pallas kernels, attend(): pl.pallas_call(attend_kernel, grid=(images,), in_specs=[image_block(PAD,...  12.7 us
  transfers between devices with their start and end apart: 9, of which 5 were waited for; matrix products, arithmetic and copies ran while one was open for 24% of the time, Pallas kernels for 2%

profile of v1, /device:TPU:0, one launch (start us, length us, event | category | flops | bytes accessed | tf_op | source)
XLA Modules:
  0.0 578.4 jit_solution(16477754538073610222)
XLA Ops:
  17.0 4.7 reshape.308
  23.1 56.0 %all-gather.3.cloned.1.call-done = bf16[768,1664]{1,0:T(8,128)(2,1)} async-done(((bf16[48,1664]{1,0:T(8,128)(2,1)}), bf16[768,1664]{1,0:T(8,128)(2,1)}) %all-gather.3.cloned.1.call-update) | async-done | bytes 2555920 | tf_op jit(solution)/shard_map/all_gather | solution.py:196
  99.0 5.4 fusion.11
  104.4 12.7 %shard_map.211 = (bf16[8,208,768]{2,1,0:T(8,128)(2,1)S(1)}, f32[8,16,208]{2,1,0:T(8,128)S(1)}) custom-call(bf16[8,208,1152]{2,1,0:T(8,128)(2,1)S(1)} %bitcast.106, bf16[8,208,1152]{2,1,0:T(8,128)(2,1)S(1)} %bitcast.108), custom_call_target="tpu_custom_call" | custom-call | flops 4253024256 | bytes 10223616 | tf_op jit(solution)/shard_map/pallas_call | solution.py:109
  121.8 40.3 %all-gather.5.cloned.1.call-done = bf16[768,3072]{1,0:T(8,128)(2,1)} async-done(((bf16[48,3072]{1,0:T(8,128)(2,1)}), bf16[768,3072]{1,0:T(8,128)(2,1)}) %all-gather.5.cloned.1.call-update) | async-done | bytes 4718608 | tf_op jit(solution)/shard_map/all_gather | solution.py:197
  167.9 6.6 %multiply_convert_fusion.3 = (bf16[1664,1536]{1,0:T(8,128)(2,1)}, f32[1664,1536]{1,0:T(8,128)S(1)}) fusion(f32[1536]{0:T(1024)S(1)} %get-tuple-element.100, bf16[1664,768]{1,0:T(8,128)(2,1)S(1)} %add_convert_fusion.1, bf16[768,3072]{1,0:T(8,128)(2,1)S(1)} %copy-done.27), kind=kOutput, calls=%fused_computation.18 | convolution fusion | flops 3941203968 | bytes 20258816 | tf_op jit(solution)/shard_map/dot_general | solution.py:22
  174.6 8.7 %convert_reduce_fusion.1 = (bf16[1536]{0:T(1024)(128)(2,1)S(1)}, bf16[1664,1536]{1,0:T(8,128)(2,1)}) fusion(f32[1664,1536]{1,0:T(8,128)S(1)} %get-tuple-element.110, f32[1536]{0:T(1024)S(1)} %get-tuple-element.100, bf16[1664,768]{1,0:T(8,128)(2,1)S(1)} %bitcast.115, bf16[768,3072]{1,0:T(8,128)(2,1)S(1)} %copy-done.27), kind=kOutput, calls=%fused_computation.13 | convolution fusion | flops 3964205568 | bytes 20261888 | tf_op jit(solution)/shard_map/dot_general | solution.py:22
  183.6 9.8 %fusion.41 = f32[1664,768]{1,0:T(8,128)} fusion(bf16[1664,1536]{1,0:T(8,128)(2,1)} %get-tuple-element.116, bf16[768,3072]{1,0:T(8,128)(2,1)} %all-gather.5.cloned.1.call-done), kind=kOutput, calls=%fused_computation.80 | convolution fusion | flops 3925868544 | bytes 12582912 | tf_op jit(solution)/shard_map/dot_general | solution.py:22
  193.4 9.7 %multiply_convert_fusion.2 = (bf16[1664,1536]{1,0:T(8,128)(2,1)}, f32[1664,1536]{1,0:T(8,128)}) fusion(f32[1536]{0:T(1024)S(1)} %get-tuple-element.99, bf16[1664,768]{1,0:T(8,128)(2,1)S(1)} %copy-done.19, bf16[768,3072]{1,0:T(8,128)(2,1)} %collective-permute-done.1), kind=kOutput, calls=%fused_computation.16 | convolution fusion | flops 3941203968 | bytes 20256768 | tf_op jit(solution)/shard_map/dot_general | solution.py:22
  203.1 10.7 %convert_reduce_fusion = (bf16[1536]{0:T(1024)(128)(2,1)S(1)}, bf16[1664,1536]{1,0:T(8,128)(2,1)S(1)}) fusion(f32[1664,1536]{1,0:T(8,128)} %get-tuple-element.112, f32[1536]{0:T(1024)S(1)} %get-tuple-element.99, bf16[1664,768]{1,0:T(8,128)(2,1)S(1)} %bitcast.116, bf16[768,3072]{1,0:T(8,128)(2,1)} %collective-permute-done.1), kind=kOutput, calls=%fused_computation.12 | convolution fusion | flops 3964205568 | bytes 20259840 | tf_op jit(solution)/shard_map/dot_general | solution.py:22
  213.9 10.9 %multiply_reduce_fusion = (bf16[768]{0:T(1024)(128)(2,1)S(1)}, f32[1664]{0:T(1024)S(1)}, f32[1664]{0:T(1024)S(1)}, bf16[768]{0:T(1024)(128)(2,1)S(1)}, f32[1664,768]{1,0:T(8,128)S(1)}) fusion(f32[1664,768]{1,0:T(8,128)S(1)} %bitcast.114, f32[1664]{0:T(1024)S(1)} %add_rsqrt_fusion, f32[1664]{0:T(1024)S(1)} %broadcast_multiply_fusion.4, ...), kind=kOutput, calls=%fused_computation.51 | convolution fusion | flops 3938643200 | bytes 22839296 | tf_op jit(solution)/shard_map/dot_general | solution.py:22
  232.1 29.9 %shard_map.212 = (bf16[8,208,1152]{2,1,0:T(8,128)(2,1)S(1)}, bf16[8,208,1152]{2,1,0:T(8,128)(2,1)S(1)}) custom-call(bf16[8,208,1152]{2,1,0:T(8,128)(2,1)S(1)} %bitcast.107, bf16[8,208,1152]{2,1,0:T(8,128)(2,1)S(1)} %bitcast.109, bf16[8,208,768]{2,1,0:T(8,128)(2,1)S(1)} %bitcast.112, f32[8,16,208]{2,1,0:T(8,128)S(1)} %get-tuple-element.17.lse_ref), custom_call_target="tpu_custom_call" | custom-call | flops 10632560640 | bytes 17891328 | tf_op jit(solution)/shard_map/pallas_call | solution.py:131
  262.7 5.5 fusion.32
  272.9 6.3 %fusion.47 = f32[1664,768]{1,0:T(8,128)S(1)} fusion(bf16[1664,1152]{1,0:T(8,128)(2,1)} %bitcast.104, bf16[768,1664]{1,0:T(8,128)(2,1)} %all-gather.3.cloned.1.call-done), kind=kOutput, calls=%fused_computation.86 | convolution fusion | flops 2944401408 | bytes 10715136 | tf_op jit(solution)/shard_map/dot_general | solution.py:22
  279.3 8.7 %fusion.31 = (bf16[768]{0:T(1024)(128)(2,1)S(1)}, f32[1664]{0:T(1024)S(1)}, f32[1664]{0:T(1024)S(1)}, bf16[768]{0:T(1024)(128)(2,1)S(1)}, f32[1664,768]{1,0:T(8,128)}) fusion(f32[1664]{0:T(1024)S(1)} %rsqrt.21, f32[1664]{0:T(1024)S(1)} %div.27, bf16[8,197,768]{2,1,0:T(8,128)(2,1)S(1)} %copy-done.10, f32[768]{0:T(1024)S(1)} %get-tuple-element.82, ...), kind=kOutput, calls=%fused_computation.50 | convolution fusion | flops 2958454016 | bytes 18280448 | tf_op jit(solution)/shard_map/dot_general | solution.py:22
  298.9 7.8 %convolution_convert_fusion.2 = bf16[768,1536]{1,0:T(8,128)(2,1)S(1)} fusion(bf16[1664,768]{1,0:T(8,128)(2,1)} %copy-done.18, bf16[1664,1536]{1,0:T(8,128)(2,1)} %copy-done.28), kind=kOutput, calls=%fused_computation.70 | convolution fusion | flops 3927048192 | bytes 10027008 | tf_op jit(solution)/shard_map/dot_general | solution.py:22
  307.2 7.6 %convolution_convert_fusion.1 = bf16[768,1536]{1,0:T(8,128)(2,1)S(1)} fusion(bf16[1664,768]{1,0:T(8,128)(2,1)S(1)} %bitcast.117, bf16[1664,1536]{1,0:T(8,128)(2,1)} %get-tuple-element.111), kind=kOutput, calls=%fused_computation.69 | convolution fusion | flops 3927048192 | bytes 10027008 | tf_op jit(solution)/shard_map/dot_general | solution.py:22
  315.1 4.8 add_convert_fusion.3
  319.9 4.8 add_convert_fusion.2
  327.4 9.9 %fusion.39 = f32[1664,768]{1,0:T(8,128)} fusion(bf16[1664,1536]{1,0:T(8,128)(2,1)} %get-tuple-element.109, bf16[768,3072]{1,0:T(8,128)(2,1)} %all-gather.5.cloned.1.call-done), kind=kOutput, calls=%fused_computation.78 | convolution fusion | flops 3925868544 | bytes 12582912 | tf_op jit(solution)/shard_map/dot_general | solution.py:22
  337.3 5.3 fusion.30
  344.9 10.5 %add_convert_fusion = bf16[1664,768]{1,0:T(8,128)(2,1)S(1)} fusion(f32[1664,768]{1,0:T(8,128)} %get-tuple-element.108, f32[1664,768]{1,0:T(8,128)} %fusion.39, bf16[1664,1536]{1,0:T(8,128)(2,1)} %get-tuple-element.111, f32[768]{0:T(1024)S(1)} %copy-done.26, bf16[768,3072]{1,0:T(8,128)(2,1)} %collective-permute-done.1), kind=kOutput, calls=%fused_computation.54 | convolution fusion | flops 3930980352 | bytes 20253696 | tf_op jit(solution)/shard_map/dot_general | solution.py:22
  357.8 69.4 %reduce-scatter.3.cloned.1.call-done = bf16[48,1664]{1,0:T(8,128)(2,1)} async-done(((bf16[768,1664]{1,0:T(8,128)(2,1)}), bf16[48,1664]{1,0:T(8,128)(2,1)}) %reduce-scatter.3.cloned.1.call-update) | async-done | bytes 159760 | tf_op jit(solution)/shard_map/reduce_scatter | solution.py:310
  433.0 136.8 %reduce-scatter.5.cloned.1.call-done = bf16[48,3072]{1,0:T(8,128)(2,1)} async-done(((bf16[768,3072]{1,0:T(8,128)(2,1)}), bf16[48,3072]{1,0:T(8,128)(2,1)}) %reduce-scatter.5.cloned.1.call-update) | async-done | bytes 294928 | tf_op jit(solution)/shard_map/reduce_scatter | solution.py:267
  (182 shorter events, 80.6 us)
Async XLA Ops:
  7.2 71.9 %all-gather.3.cloned.1.call-start = ((), (), s32[]{:S(2)}) async-start(), calls=%async_computation.2 | async-start | bytes 2715648 | tf_op jit(solution)/shard_map/all_gather | solution.py:196
  12.8 149.3 %all-gather.5.cloned.1.call-start = ((), (), s32[]{:S(2)}) async-start(), calls=%async_computation.3 | async-start | bytes 5013504 | tf_op jit(solution)/shard_map/all_gather | solution.py:197
  14.6 412.7 %reduce-scatter.3.cloned.1.call-start = ((), (), s32[]{:S(2)}) async-start(), calls=%async_computation.4 | async-start | bytes 2715648 | tf_op jit(solution)/shard_map/reduce_scatter | solution.py:310
  17.0 74.9 %copy-start.8 = (bf16[8,197,768]{2,1,0:T(8,128)(2,1)}, bf16[8,197,768]{2,1,0:T(8,128)(2,1)S(1)}, u32[]{:S(2)}) copy-start(bf16[8,197,768]{2,1,0:T(8,128)(2,1)S(1)} %reshape.300) | copy-start | bytes 7262212
  82.4 15.0 %collective-permute-start = (bf16[768,1536]{1,0:T(8,128)(2,1)}, bf16[768,1536]{1,0:T(8,128)(2,1)}, u32[]{:S(2)}, u32[]{:S(2)}) collective-permute-start(bf16[768,1536]{1,0:T(8,128)(2,1)} %slice.190), channel_id=1, source_target_pairs={{0,1},{1,0},{2,3},{3,2},{4,5},{5,4},{6,7},{7,6},{8,9},{9,8},{10,11... | collective-permute-start | bytes 7077896 | tf_op jit(solution)/shard_map/ppermute | solution.py:162
  99.0 18.2 %copy-start.22 = (bf16[768,384]{1,0:T(8,128)(2,1)}, bf16[768,384]{1,0:T(8,128)(2,1)S(1)}, u32[]{:S(2)}) copy-start(bf16[768,384]{1,0:T(8,128)(2,1)S(1)} %slice.193) | copy-start | bytes 1769476
  104.4 12.8 %copy-start.6 = (bf16[1664,1152]{1,0:T(8,128)(2,1)}, bf16[1664,1152]{1,0:T(8,128)(2,1)S(1)}, u32[]{:S(2)}) copy-start(bf16[1664,1152]{1,0:T(8,128)(2,1)S(1)} %fusion.11) | copy-start | bytes 11501572
  104.4 12.8 %copy-start.21 = (bf16[8,208,768]{2,1,0:T(8,128)(2,1)S(1)}, bf16[8,208,768]{2,1,0:T(8,128)(2,1)}, u32[]{:S(2)}) copy-start(bf16[8,208,768]{2,1,0:T(8,128)(2,1)} %pad.16) | copy-start | bytes 7667716
  162.1 31.3 %collective-permute-start.1 = (bf16[768,3072]{1,0:T(8,128)(2,1)}, bf16[768,3072]{1,0:T(8,128)(2,1)}, u32[]{:S(2)}, u32[]{:S(2)}) collective-permute-start(bf16[768,3072]{1,0:T(8,128)(2,1)} %all-gather.5.cloned.1.call-done), channel_id=1, source_target_pairs={{0,1},{1,0},{2,3},{3,2},{4,5},{5,4},{6,7},{7,6},{8,9},{9,8},{10,11... | collective-permute-start | bytes 14155784 | tf_op jit(solution)/shard_map/ppermute | solution.py:162
  183.6 9.8 %copy-start.19 = (bf16[1664,768]{1,0:T(8,128)(2,1)S(1)}, bf16[1664,768]{1,0:T(8,128)(2,1)}, u32[]{:S(2)}) copy-start(bf16[1664,768]{1,0:T(8,128)(2,1)} %copy-done.18) | copy-start | bytes 7667716
  193.4 9.8 %copy-start.14 = (bf16[8,208,768]{2,1,0:T(8,128)(2,1)S(1)}, bf16[8,208,768]{2,1,0:T(8,128)(2,1)}, u32[]{:S(2)}) copy-start(bf16[8,208,768]{2,1,0:T(8,128)(2,1)} %get-tuple-element.79) | copy-start | bytes 7667716
  193.4 20.4 %slice-start = ((s8[5111808]{0:T(1024)(128)(4,1)}), s8[4194304]{0:T(1024)(128)(4,1)S(1)}, s32[]{:S(2)}) async-start(s8[5111808]{0:T(1024)(128)(4,1)} %bitcast.113), calls=%async_computation.6 | async-start | bytes 8388608
  203.1 10.7 %slice-start.1 = ((s8[5111808]{0:T(1024)(128)(4,1)}), s8[917504]{0:T(1024)(128)(4,1)S(1)}, s32[]{:S(2)}) async-start(s8[5111808]{0:T(1024)(128)(4,1)} %bitcast.113), calls=%async_computation.7 | async-start | bytes 1835008
  213.8 10.9 %copy-start.28 = (bf16[1664,1536]{1,0:T(8,128)(2,1)}, bf16[1664,1536]{1,0:T(8,128)(2,1)S(1)}, u32[]{:S(2)}) copy-start(bf16[1664,1536]{1,0:T(8,128)(2,1)S(1)} %get-tuple-element.118) | copy-start | bytes 15335428
  227.0 41.1 %copy-start.12 = (f32[1664,768]{1,0:T(8,128)}, f32[1664,768]{1,0:T(8,128)S(1)}, u32[]{:S(2)}) copy-start(f32[1664,768]{1,0:T(8,128)S(1)} %get-tuple-element.77) | copy-start | bytes 15335428
  232.1 30.6 %copy-start.9 = (bf16[8,197,768]{2,1,0:T(8,128)(2,1)S(1)}, bf16[8,197,768]{2,1,0:T(8,128)(2,1)}, u32[]{:S(2)}) copy-start(bf16[8,197,768]{2,1,0:T(8,128)(2,1)} %copy-done.8) | copy-start | bytes 7262212
  262.1 9.9 %copy-start = (bf16[8,208,1152]{2,1,0:T(8,128)(2,1)}, bf16[8,208,1152]{2,1,0:T(8,128)(2,1)S(1)}, u32[]{:S(2)}) copy-start(bf16[8,208,1152]{2,1,0:T(8,128)(2,1)S(1)} %get-tuple-element.18) | copy-start | bytes 11501572
  291.6 5.2 collective-permute-start.2
  298.8 271.0 %reduce-scatter.5.cloned.1.call-start = ((), (), s32[]{:S(2)}) async-start(), calls=%async_computation.5 | async-start | bytes 5013504 | tf_op jit(solution)/shard_map/reduce_scatter | solution.py:267
  298.8 16.2 %slice-start.5 = ((s8[5111808]{0:T(1024)(128)(4,1)}), s8[4194304]{0:T(1024)(128)(4,1)S(1)}, s32[]{:S(2)}) async-start(s8[5111808]{0:T(1024)(128)(4,1)} %bitcast.129), calls=%async_computation.11 | async-start | bytes 8388608
  306.7 8.3 %collective-permute-start.3 = (bf16[768,1536]{1,0:T(8,128)(2,1)S(1)}, bf16[768,1536]{1,0:T(8,128)(2,1)S(1)}, u32[]{:S(2)}, u32[]{:S(2)}) collective-permute-start(bf16[768,1536]{1,0:T(8,128)(2,1)S(1)} %convolution_convert_fusion.2), channel_id=1, source_target_pairs={{0,1},{1,0},{2,3},{3,2},{4,5},{5,4},{6,7},{7,6},{8,9},{9,8},{10,11... | collective-permute-start | bytes 7077896 | tf_op jit(solution)/shard_map/ppermute | solution.py:162
  307.2 12.7 %slice-start.3 = ((s8[5111808]{0:T(1024)(128)(4,1)}), s8[4194304]{0:T(1024)(128)(4,1)S(1)}, s32[]{:S(2)}) async-start(s8[5111808]{0:T(1024)(128)(4,1)} %bitcast.127), calls=%async_computation.9 | async-start | bytes 8388608
  307.2 12.7 %slice-start.4 = ((s8[5111808]{0:T(1024)(128)(4,1)}), s8[917504]{0:T(1024)(128)(4,1)S(1)}, s32[]{:S(2)}) async-start(s8[5111808]{0:T(1024)(128)(4,1)} %bitcast.127), calls=%async_computation.10 | async-start | bytes 1835008
  314.8 5.1 collective-permute-start.4
  (21 other events, 109.8 us)
Sparse Core Ops, SparseCore 0:
  12.9 66.0 all-gather.2
  82.4 79.6 all-gather.4
  298.9 128.2 reduce-scatter.2
  433.1 136.6 reduce-scatter.4
